TPU v7x, 32 devices: a whole 2x2x4 slice. The times are simulated.
32 devices in a mesh: group: 2 (over x), freq: 16 (over z, y, core).
Axes of the slice: x: 2, y: 2, z: 4, core: 2. Of those that a mesh axis runs over, the one named last changes fastest.
Arguments:
- slip_history: float32 [512, 3, 16384], P('freq', None, 'group'), parts along dimension 2, may hold values from -6 to 6
- frequency_ids: int32 [16], replicated, may hold values from 0 to 256, as said below
- col_clusters: int32 [64, 8], replicated, may hold values from 0 to 63, as said below
- basis_ranks: int32 [16, 128], P('freq', 'group'), parts along dimension 1, may hold values from 8 to 32
- left_basis: bfloat16 [16, 128, 2, 32, 3, 128], P('freq', 'group'), parts along dimension 1, may hold values from -0.75 to 0.75
- right_basis: bfloat16 [16, 128, 2, 32, 3, 128], P('freq', 'group'), parts along dimension 1, may hold values from -0.21875 to 0.21875
- coupling: bfloat16 [16, 128, 8, 2, 1024], P('freq', 'group'), parts along dimension 1, may hold values from -0.25 to 0.25
Outputs:
- traction: float32 [512, 3, 16384], P('freq', None, 'group'), parts along dimension 2
There are 2 independent parts, one for each index of `group`. A program takes and returns all parts, laid end to end along the dimension named above; an argument that names none is the same for every part. Nothing has to cross between parts.
Inputs may be any that keep to these rules, and one draw needn't show every extreme that they name: `frequency_ids`: distinct frequency numbers; 0 and 256 are always among them. `col_clusters`: each row a lists 8 distinct clusters, the first of them a itself.
All inputs are finite; a program needn't handle non-finite values.
Results may differ from a plain program's by a relative error of at most 0.0057.
Values may be sent and summed in bfloat16 or wider, within the bound.
A program may use at most 128 MiB of HBM per device.

v0:
```python
import functools
import math

import jax
import jax.numpy as jnp
from jax import lax
from jax.experimental import pallas as pl
from jax.experimental.pallas import tpu as pltpu
from jax.sharding import PartitionSpec as P

STEPS = 512
DAMPING = 0.5
LEAF = 128
CHUNKS = 8
MESH = pl.DeviceIdType.MESH
MIB = 1024 * 1024


def split_f32(x):
    hi = x.astype(jnp.bfloat16)
    lo = (x - hi.astype(jnp.float32)).astype(jnp.bfloat16)
    return hi, lo


def forward_matrix(frequency_ids, time_ids):
    phases = frequency_ids[:, None] * time_ids[None, :] % STEPS
    angles = phases.astype(jnp.float32) * (2.0 * math.pi / STEPS)
    weights = DAMPING ** (time_ids.astype(jnp.float32) / STEPS)
    table = jnp.stack([weights[None, :] * jnp.cos(angles), -weights[None, :] * jnp.sin(angles)], axis=1)
    hi, lo = split_f32(table)
    eye = jnp.eye(CHUNKS, dtype=jnp.bfloat16)
    rows = table.shape[0] * 2 * CHUNKS
    spread = lambda part: (part[:, :, None, None, :] * eye[None, None, :, :, None]).reshape(rows, -1)
    return jnp.concatenate([spread(hi), spread(hi), spread(lo)], axis=1)


def inverse_matrix(frequency_ids, time_ids):
    phases = time_ids[:, None] * frequency_ids[None, :] % STEPS
    angles = phases.astype(jnp.float32) * (2.0 * math.pi / STEPS)
    scales = DAMPING ** (-time_ids.astype(jnp.float32) / STEPS) / STEPS
    doubled = jnp.where((frequency_ids == 0) | (frequency_ids == STEPS // 2), 1.0, 2.0)
    factor = scales[:, None] * doubled[None, :]
    table = jnp.stack([factor * jnp.cos(angles), -factor * jnp.sin(angles)], axis=2)
    hi, lo = split_f32(table)
    eye = jnp.eye(CHUNKS, dtype=jnp.bfloat16)
    rows = table.shape[0] * CHUNKS
    spread = lambda part: (part[None, :, :, :, None] * eye[:, None, None, None, :]).reshape(rows, -1)
    return spread(hi), spread(lo)


def place(zs, ys):
    me = lax.axis_index("freq")
    core = lax.rem(me, 2)
    y = lax.rem(me // 2, ys)
    z = me // (2 * ys)
    return z, y, core


def index_of(z, y, core, ys):
    return (z * ys + y) * 2 + core


def greet(targets):
    barrier = pltpu.get_barrier_semaphore()
    for target in targets:
        pl.semaphore_signal(barrier, inc=1, device_id={"freq": target}, device_id_type=MESH)
    return lambda: pl.semaphore_wait(barrier, len(targets))


def partners(z, y, core, zs, ys):
    targets = [index_of(z, y, 1 - core, ys)]
    targets += [index_of(z, lax.rem(y + s, ys), core, ys) for s in range(1, ys)]
    targets += [index_of(lax.rem(z + s, zs), y, core, ys) for s in range(1, zs)]
    return targets


def scatter_kernel(zs, ys, table_ref, slip_ref, out_ref, acc, send0, recv0, send1, recv1, send2, recv2, *sems):
    ss0, rs0, ss1, rs1, ss2, rs2 = sems
    z, y, core = place(zs, ys)
    ready = greet(partners(z, y, core, zs, ys))
    times, width = slip_ref.shape[1], slip_ref.shape[2] // CHUNKS
    order = list(range(zs // 2, zs // 2 - zs, -1))
    order = [s % zs for s in order if s % zs] + [0]
    for j in range(3):
        x = jnp.concatenate([slip_ref[j, :, c * width:(c + 1) * width] for c in range(CHUNKS)], axis=0)
        hi, lo = split_f32(x)
        stack = jnp.concatenate([hi, lo, hi], axis=0)
        res = jnp.dot(table_ref[...], stack, preferred_element_type=jnp.float32)
        res = res.reshape(zs * ys, 2, 2 * CHUNKS, width)
        first, second = res[:, 0], res[:, 1]
        own = jnp.where(core == 0, first, second)
        other = jnp.where(core == 0, second, first)
        acc[:, j] = own
        send0[:, j] = other.astype(jnp.bfloat16)
    ready()
    stage0 = {}
    for s in order:
        at = lax.rem(z + s, zs)
        rows = pl.ds(at * ys, ys)
        stage0[s] = pltpu.make_async_remote_copy(
            src_ref=send0.at[rows], dst_ref=recv0.at[rows], send_sem=ss0.at[s], recv_sem=rs0.at[s],
            device_id={"freq": index_of(z, y, 1 - core, ys)}, device_id_type=MESH)
        stage0[s].start()
    stage1, stage2 = {}, {}
    for s in order:
        at = lax.rem(z + s, zs)
        stage0[s].wait_recv()
        for step in range(1, ys):
            there = lax.rem(y + step, ys)
            block = at * ys + there
            send1[step - 1, at] = (acc[block] + recv0[block].astype(jnp.float32)).astype(jnp.bfloat16)
            stage1[s, step] = pltpu.make_async_remote_copy(
                src_ref=send1.at[step - 1, at], dst_ref=recv1.at[step - 1, at],
                send_sem=ss1.at[step - 1, s], recv_sem=rs1.at[step - 1, s],
                device_id={"freq": index_of(z, there, core, ys)}, device_id_type=MESH)
            stage1[s, step].start()
    for s in order:
        at = lax.rem(z + s, zs)
        block = at * ys + y
        total = acc[block] + recv0[block].astype(jnp.float32)
        for step in range(1, ys):
            stage1[s, step].wait_recv()
            total += recv1[step - 1, at].astype(jnp.float32)
        if s:
            send2[s - 1] = total.astype(jnp.bfloat16)
            stage2[s] = pltpu.make_async_remote_copy(
                src_ref=send2.at[s - 1], dst_ref=recv2.at[s - 1], send_sem=ss2.at[s - 1], recv_sem=rs2.at[s - 1],
                device_id={"freq": index_of(at, y, core, ys)}, device_id_type=MESH)
            stage2[s].start()
    for s in order[:-1]:
        stage2[s].wait_recv()
        total += recv2[s - 1].astype(jnp.float32)
    out_ref[...] = total.astype(jnp.bfloat16)
    for copies in (stage0, stage1, stage2):
        for copy in copies.values():
            copy.wait_send()


def scatter_spectra(table, slip, zs, ys):
    block = (3, 2 * CHUNKS, slip.shape[2] // CHUNKS)
    bf16 = jnp.bfloat16
    high, many = max(ys - 1, 1), max(zs - 1, 1)
    return pl.pallas_call(
        functools.partial(scatter_kernel, zs, ys),
        out_shape=jax.ShapeDtypeStruct(block, bf16),
        in_specs=[pl.BlockSpec(memory_space=pltpu.VMEM)] * 2,
        out_specs=pl.BlockSpec(memory_space=pltpu.VMEM),
        scratch_shapes=[
            pltpu.VMEM((zs * ys,) + block, jnp.float32),
            pltpu.VMEM((zs * ys,) + block, bf16),
            pltpu.VMEM((zs * ys,) + block, bf16),
            pltpu.VMEM((high, zs) + block, bf16),
            pltpu.VMEM((high, zs) + block, bf16),
            pltpu.VMEM((many,) + block, bf16),
            pltpu.VMEM((many,) + block, bf16),
            pltpu.SemaphoreType.DMA((zs,)),
            pltpu.SemaphoreType.DMA((zs,)),
            pltpu.SemaphoreType.DMA((high, zs)),
            pltpu.SemaphoreType.DMA((high, zs)),
            pltpu.SemaphoreType.DMA((many,)),
            pltpu.SemaphoreType.DMA((many,)),
        ],
        compiler_params=pltpu.CompilerParams(collective_id=0, has_side_effects=True, vmem_limit_bytes=48 * MIB),
        name="spectra_scatter",
    )(table, slip)


def operator_kernel(spec_ref, right_ref, coupling_ref, left_ref, rank_ref, col_ref, image_ref, coef, tiled, sums):
    f32, bf16 = jnp.float32, jnp.bfloat16
    groups = spec_ref.shape[2] // LEAF
    rank = right_ref.shape[3]
    clusters = groups * CHUNKS
    blocks = coupling_ref.shape[1]
    chunk_row = lax.broadcasted_iota(jnp.int32, (2 * CHUNKS, 2 * rank), 0) % CHUNKS
    half = CHUNKS // 2
    for g in range(groups):
        lanes = slice(g * LEAF, (g + 1) * LEAF)
        x = jnp.concatenate([spec_ref[j, :, lanes] for j in range(3)], axis=1)
        prod = jnp.zeros((2 * CHUNKS, 2 * rank), f32)
        for h in range(2):
            basis = jnp.concatenate(
                [jnp.concatenate([right_ref[(h * half + c) * groups + g, q, j] for c in range(half) for q in range(2)], axis=0)
                 for j in range(3)], axis=1)
            full = lax.dot_general(x, basis, (((1,), (1,)), ((), ())), preferred_element_type=f32)
            for c in range(half):
                prod = jnp.where(chunk_row == h * half + c, full[:, c * 2 * rank:(c + 1) * 2 * rank], prod)
        low, high = prod[:CHUNKS], prod[CHUNKS:]
        rows = slice(g * CHUNKS, (g + 1) * CHUNKS)
        coef[0, rows] = low[:, :rank] - high[:, rank:]
        coef[1, rows] = high[:, :rank] + low[:, rank:]
    kept = lax.broadcasted_iota(jnp.int32, (clusters, rank), 1) < rank_ref[...]
    area = rank * rank
    lane_of = lax.broadcasted_iota(jnp.int32, (rank, area), 1)
    spread = (lane_of % rank == lax.broadcasted_iota(jnp.int32, (rank, area), 0)).astype(bf16)
    for p in range(2):
        held = jnp.where(kept, coef[p], 0.0).astype(bf16)
        tiled[p] = jnp.dot(held, spread, preferred_element_type=f32)

    def couple(step, carry):
        found = [[], []]
        for r in range(4):
            a = step * 4 + r
            totals = [jnp.zeros((2, area), f32), jnp.zeros((2, area), f32)]
            for i in range(blocks):
                source = col_ref[a, i]
                row = (source % groups) * CHUNKS + source // groups
                block = coupling_ref[a, i].astype(f32)
                for p in range(2):
                    totals[p] = totals[p] + block * tiled[p, pl.ds(row, 1), :]
            found[0].append(totals[0])
            found[1].append(totals[1])
        for p in range(2):
            sums[p, pl.ds(pl.multiple_of(step * 8, 8), 8), :] = jnp.concatenate(found[p], axis=0)
        return carry

    lax.fori_loop(0, clusters // 4, couple, 0)
    row_of = lax.broadcasted_iota(jnp.int32, (area, rank), 0)
    gather = (row_of // rank == lax.broadcasted_iota(jnp.int32, (area, rank), 1)).astype(bf16)
    target = lax.broadcasted_iota(jnp.int32, (clusters, 2 * clusters), 0)
    origin = lax.broadcasted_iota(jnp.int32, (clusters, 2 * clusters), 1)
    cluster = (target % CHUNKS) * groups + target // CHUNKS
    picks = [(origin == 2 * cluster + q).astype(f32) for q in range(2)]
    parts = {}
    for p in range(2):
        hi, lo = split_f32(sums[p])
        short = jnp.dot(hi, gather, preferred_element_type=f32) + jnp.dot(lo, gather, preferred_element_type=f32)
        for q in range(2):
            parts[p, q] = jnp.dot(picks[q], short, precision=lax.Precision.HIGHEST, preferred_element_type=f32)
    real = jnp.where(kept, parts[0, 0] - parts[1, 1], 0.0)
    imag = jnp.where(kept, parts[1, 0] + parts[0, 1], 0.0)
    for g in range(groups):
        rows = slice(g * CHUNKS, (g + 1) * CHUNKS)
        mixed = jnp.concatenate([
            jnp.concatenate([real[rows], -imag[rows]], axis=1),
            jnp.concatenate([imag[rows], real[rows]], axis=1)], axis=0)
        masked = jnp.concatenate([jnp.where(chunk_row == c, mixed, 0.0) for c in range(CHUNKS)], axis=1).astype(bf16)
        for j in range(3):
            basis = jnp.concatenate([left_ref[c * groups + g, q, j] for c in range(CHUNKS) for q in range(2)], axis=0)
            out = jnp.dot(masked, basis, preferred_element_type=f32)
            image_ref[j, :, g * LEAF:(g + 1) * LEAF] = out.astype(bf16)


def apply_operator(spectrum, right, coupling, left, ranks, col_clusters):
    clusters, rank = right.shape[0], right.shape[3]
    groups = clusters // CHUNKS
    order = ranks.reshape(CHUNKS, groups).T.reshape(clusters, 1)
    vmem = pl.BlockSpec(memory_space=pltpu.VMEM)
    return pl.pallas_call(
        operator_kernel,
        out_shape=jax.ShapeDtypeStruct(spectrum.shape, jnp.bfloat16),
        in_specs=[vmem] * 5 + [pl.BlockSpec(memory_space=pltpu.SMEM)],
        out_specs=vmem,
        scratch_shapes=[
            pltpu.VMEM((2, clusters, rank), jnp.float32),
            pltpu.VMEM((2, clusters, rank * rank), jnp.float32),
            pltpu.VMEM((2, 2 * clusters, rank * rank), jnp.float32),
        ],
        compiler_params=pltpu.CompilerParams(vmem_limit_bytes=40 * MIB),
        name="operator",
    )(spectrum, right, coupling, left, order, col_clusters)


def gather_kernel(zs, ys, image_ref, out_ref, local_sem, *sems):
    zsend, zrecv, ysend, yrecv, csend, crecv = sems
    z, y, core = place(zs, ys)
    ready = greet(partners(z, y, core, zs, ys))
    me = index_of(z, y, core, ys)
    mine = pltpu.make_async_copy(image_ref, out_ref.at[me], local_sem)
    mine.start()
    ready()
    copies = []

    def send(block, source, target, send_sem, recv_sem):
        copy = pltpu.make_async_remote_copy(
            src_ref=source, dst_ref=out_ref.at[block], send_sem=send_sem, recv_sem=recv_sem,
            device_id={"freq": target}, device_id_type=MESH)
        copy.start()
        copies.append(copy)
        return copy

    other = index_of(z, y, 1 - core, ys)
    order = [s % zs for s in range(zs // 2, zs // 2 - zs, -1) if s % zs]
    for s in order:
        send(me, image_ref, index_of(lax.rem(z + s, zs), y, core, ys), zsend.at[s - 1], zrecv.at[s - 1])
    for step in range(1, ys):
        send(me, image_ref, index_of(z, lax.rem(y + step, ys), core, ys), ysend.at[step - 1, 0], yrecv.at[step - 1, 0])
    send(me, image_ref, other, csend.at[0, 0], crecv.at[0, 0])

    def arrived(block, recv_sem):
        pltpu.make_async_copy(out_ref.at[block], out_ref.at[block], recv_sem).wait()

    near = sorted(range(1, zs), key=lambda s: min(s, zs - s))
    for s in near:
        block = index_of(lax.rem(z + zs - s, zs), y, core, ys)
        arrived(block, zrecv.at[s - 1])
        for step in range(1, ys):
            send(block, out_ref.at[block], index_of(z, lax.rem(y + step, ys), core, ys),
                 ysend.at[step - 1, s], yrecv.at[step - 1, s])
        send(block, out_ref.at[block], other, csend.at[0, s], crecv.at[0, s])
    for s in [0] + near:
        for step in range(1, ys):
            block = index_of(lax.rem(z + zs - s, zs), lax.rem(y + ys - step, ys), core, ys)
            arrived(block, yrecv.at[step - 1, s])
            send(block, out_ref.at[block], other, csend.at[step, s], crecv.at[step, s])
    for s in [0] + near:
        for step in range(ys):
            block = index_of(lax.rem(z + zs - s, zs), lax.rem(y + ys - step, ys), 1 - core, ys)
            arrived(block, crecv.at[step, s])
    mine.wait()
    for copy in copies:
        copy.wait_send()


def gather_images(image, zs, ys):
    high, many = max(ys - 1, 1), max(zs - 1, 1)
    vmem = pl.BlockSpec(memory_space=pltpu.VMEM)
    return pl.pallas_call(
        functools.partial(gather_kernel, zs, ys),
        out_shape=jax.ShapeDtypeStruct((zs * ys * 2,) + image.shape, image.dtype),
        in_specs=[vmem],
        out_specs=vmem,
        scratch_shapes=[
            pltpu.SemaphoreType.DMA,
            pltpu.SemaphoreType.DMA((many,)),
            pltpu.SemaphoreType.DMA((many,)),
            pltpu.SemaphoreType.DMA((high, zs)),
            pltpu.SemaphoreType.DMA((high, zs)),
            pltpu.SemaphoreType.DMA((ys, zs)),
            pltpu.SemaphoreType.DMA((ys, zs)),
        ],
        compiler_params=pltpu.CompilerParams(collective_id=1, has_side_effects=True, vmem_limit_bytes=32 * MIB),
        name="image_gather",
    )(image)


def synthesis_kernel(hi_ref, lo_ref, image_ref, out_ref):
    width, times = image_ref.shape[2], out_ref.shape[1]
    x = image_ref[...].reshape(-1, width)
    res = jnp.dot(hi_ref[...], x, preferred_element_type=jnp.float32)
    res += jnp.dot(lo_ref[...], x, preferred_element_type=jnp.float32)
    for c in range(CHUNKS):
        out_ref[0, :, c * width:(c + 1) * width] = res[c * times:(c + 1) * times]


def synthesize(hi, lo, images, times):
    n, _, rows, width = images.shape
    whole = pl.BlockSpec(hi.shape, lambda j: (0, 0))
    return pl.pallas_call(
        synthesis_kernel,
        grid=(3,),
        out_shape=jax.ShapeDtypeStruct((3, times, CHUNKS * width), jnp.float32),
        in_specs=[whole, whole, pl.BlockSpec((n, None, rows, width), lambda j: (0, j, 0, 0))],
        out_specs=pl.BlockSpec((1, times, CHUNKS * width), lambda j: (j, 0, 0)),
        compiler_params=pltpu.CompilerParams(vmem_limit_bytes=32 * MIB),
        name="synthesis",
    )(hi, lo, images)


def body(zs, ys, slip_history, frequency_ids, col_clusters, basis_ranks, left_basis, right_basis, coupling):
    times = slip_history.shape[0]
    time_ids = lax.axis_index("freq") * times + jnp.arange(times, dtype=jnp.int32)
    slip = jnp.transpose(slip_history, (1, 0, 2))
    right = jnp.transpose(right_basis[0], (0, 1, 3, 2, 4))
    left = jnp.transpose(left_basis[0], (0, 1, 3, 2, 4))
    spectrum = scatter_spectra(forward_matrix(frequency_ids, time_ids), slip, zs, ys)
    image = apply_operator(spectrum, right, coupling[0], left, basis_ranks[0], col_clusters)
    images = gather_images(image, zs, ys)
    hi, lo = inverse_matrix(frequency_ids, time_ids)
    traction = synthesize(hi, lo, images, times)
    return jnp.transpose(traction, (1, 0, 2))


def solution(mesh):
    ys = max(4 // mesh.shape["group"], 1)
    zs = mesh.shape["freq"] // (2 * ys)
    return jax.shard_map(
        functools.partial(body, zs, ys),
        mesh=mesh,
        in_specs=(
            P("freq", None, "group"),
            P(),
            P(),
            P("freq", "group"),
            P("freq", "group", None, None, None, None),
            P("freq", "group", None, None, None, None),
            P("freq", "group", None, None, None),
        ),
        out_specs=P("freq", None, "group"),
        check_vma=False,
    )
```

profile of v0, /device:TPU:21, one launch (start us, length us, event | category | flops | bytes accessed | tf_op | source)
XLA Modules:
  0.0 73.6 jit_solution(9081599327892181107)
XLA Ops:
  0.0 0.0 copy-start
  0.0 0.5 broadcast.583
  0.5 1.6 %reduce.3 = s32[64]{0:T(128)S(1)} reduce(s32[1,64]{1,0:T(1,128)} %param.10, s32[]{:T(128)} %broadcast.583), dimensions={0}, to_apply=%param.10.reduce_sub_computation.3 | reduce | bytes 516 | tf_op args[3]
  2.1 0.7 or_select_fusion
  2.8 0.1 copy.20
  2.9 0.1 reshape_squeeze.3
  2.9 0.1 copy.22
  3.0 0.8 %cosine_multiply_fusion = (f32[16,1,32]{2,0,1:T(8,128)S(1)}, f32[16,1,32]{2,0,1:T(8,128)S(1)}) fusion(s32[32]{0:T(128)S(1)} %iota_add_fusion, s32[16]{0:T(128)} %param.8, f32[32]{0:T(128)S(1)} %get-tuple-element.13, f32[32]{0:T(128)S(1)} %fusion.10), kind=kLoop, calls=%fused_computation.31 | loop fusion | flops 8192 | bytes 4544 | tf_op jit(solution)/shard_map/mul | solution.py:29
  3.9 0.8 %multiply_multiply_fusion = (f32[32,16,1]{0,1,2:T(8,128)S(1)}, f32[32,16,1]{0,1,2:T(8,128)S(1)}) fusion(s32[16]{0:T(128)} %param.8, s32[32]{0:T(128)S(1)} %iota_add_fusion, f32[16]{0:T(128)S(1)} %or_select_fusion, f32[32]{0:T(128)S(1)} %get-tuple-element.14), kind=kLoop, calls=%fused_computation.22 | loop fusion | flops 9216 | bytes 4480 | tf_op jit(solution)/shard_map/mul | solution.py:43
  4.7 0.1 reshape.579.rank_ref
  4.8 0.8 %copy.24.col_ref = s32[64,8]{1,0:T(8,128)S(1)} copy(s32[64,8]{0,1:T(8,128)} %param.9) | data formatting | bytes 4096 | tf_op args[2]
  5.6 1.1 %broadcast_multiply_fusion.2 = (bf16[8,32,16,2,8]{1,0,4,3,2:T(8,128)(2,1)}, bf16[8,32,16,2,8]{1,0,4,3,2:T(8,128)(2,1)}) fusion(bf16[32,16,2]{0,2,1:T(2,128)(2,1)S(1)} %copy.18, bf16[8,8]{0,1:T(8,128)(2,1)S(1)} %fusion.9, bf16[32,16,2]{0,2,1:T(2,128)(2,1)S(1)} %copy.17), kind=kLoop, calls=%fused_computation.3 | loop fusion | flops 131072 | bytes 266368 | tf_op jit(solution)/shard_map/mul | solution.py:47
  6.7 1.4 %mul.293 = bf16[256,256]{0,1:T(8,128)(2,1)S(1)} reshape(bf16[8,32,16,2,8]{1,0,4,3,2:T(8,128)(2,1)} %get-tuple-element.7) | data formatting | bytes 262144 | tf_op jit(solution)/shard_map/mul | solution.py:47
  8.1 0.1 copy.26.lo_ref
  8.2 2.1 %mul.290 = bf16[256,256]{0,1:T(8,128)(2,1)} reshape(bf16[8,32,16,2,8]{1,0,4,3,2:T(8,128)(2,1)} %get-tuple-element.8) | data formatting | bytes 262144 | tf_op jit(solution)/shard_map/mul | solution.py:47
  10.3 1.0 %copy.25.hi_ref = bf16[256,256]{1,0:T(8,128)(2,1)S(1)} copy(bf16[256,256]{0,1:T(8,128)(2,1)} %mul.290) | data formatting | bytes 262144 | tf_op jit(solution)/shard_map/mul | solution.py:47
  11.3 1.1 %broadcast_multiply_fusion.1 = (bf16[16,2,8,8,32]{4,3,2,1,0:T(8,128)(2,1)}, bf16[16,2,8,8,32]{4,3,2,1,0:T(8,128)(2,1)}) fusion(bf16[8,8]{1,0:T(8,128)(2,1)S(1)} %copy.20, bf16[16,2,32]{2,1,0:T(2,128)(2,1)S(1)} %copy.19, bf16[16,2,32]{2,1,0:T(2,128)(2,1)S(1)} %copy.21), kind=kLoop, calls=%fused_computation.2 | loop fusion | flops 131072 | bytes 266368 | tf_op jit(solution)/shard_map/mul | solution.py:33
  12.4 2.1 %mul.306 = bf16[256,256]{1,0:T(8,128)(2,1)} reshape(bf16[16,2,8,8,32]{4,3,2,1,0:T(8,128)(2,1)} %get-tuple-element.5) | data formatting | bytes 262144 | tf_op jit(solution)/shard_map/mul | solution.py:33
  14.5 2.1 %mul.309 = bf16[256,256]{1,0:T(8,128)(2,1)} reshape(bf16[16,2,8,8,32]{4,3,2,1,0:T(8,128)(2,1)} %get-tuple-element.6) | data formatting | bytes 262144 | tf_op jit(solution)/shard_map/mul | solution.py:33
  16.6 0.0 copy-start.1
  16.6 1.2 %pad_maximum_fusion.table_ref = bf16[256,768]{1,0:T(8,128)(2,1)S(1)} fusion(bf16[256,256]{1,0:T(8,128)(2,1)} %mul.309, bf16[256,256]{1,0:T(8,128)(2,1)} %mul.306), kind=kLoop, calls=%fused_computation | loop fusion | flops 1179648 | bytes 655360 | tf_op jit(solution)/shard_map/concatenate | solution.py:34
  17.8 0.0 copy-done
  17.8 18.0 %spectra_scatter.1.spec_ref = bf16[3,16,1024]{2,1,0:T(8,128)(2,1)S(1)} custom-call(bf16[256,768]{1,0:T(8,128)(2,1)S(1)} %pad_maximum_fusion.table_ref, f32[3,32,8192]{2,1,0:T(8,128)S(1)} %bitcast.22), custom_call_target="tpu_custom_call" | custom-call | tf_op jit(solution)/shard_map/spectra_scatter/pallas_call | solution.py:143
  35.8 0.0 copy-done.1
  35.8 0.0 copy-start.2
  35.8 1.9 %copy-done.2 = bf16[1,64,2,32,3,128]{5,3,4,2,1,0:T(8,128)(2,1)S(1)} copy-done((bf16[1,64,2,32,3,128]{5,3,4,2,1,0:T(8,128)(2,1)S(1)}, bf16[1,64,2,32,3,128]{5,3,4,2,1,0:T(8,128)(2,1)}, u32[]{:S(2)}) %copy-start.2) | copy-done | bytes 3145752
  37.7 0.0 copy-start.3
  37.7 1.6 %copy-done.3 = bf16[1,64,8,2,1024]{4,3,2,1,0:T(2,128)(2,1)S(1)} copy-done((bf16[1,64,8,2,1024]{4,3,2,1,0:T(2,128)(2,1)S(1)}, bf16[1,64,8,2,1024]{4,3,2,1,0:T(2,128)(2,1)}, u32[]{:S(2)}) %copy-start.3) | copy-done | bytes 2097176
  39.3 10.7 %operator.1.image_ref = bf16[3,16,1024]{2,1,0:T(8,128)(2,1)S(1)} custom-call(bf16[3,16,1024]{2,1,0:T(8,128)(2,1)S(1)} %spectra_scatter.1.spec_ref, bf16[64,2,3,32,128]{4,3,2,1,0:T(8,128)(2,1)S(1)} %bitcast.23, bf16[64,8,2,1024]{3,2,1,0:T(2,128)(2,1)S(1)} %bitcast.25, bf16[64,2,3,32,128]{4,3,2,1,0:T(8,128)(2,1)S(1)} %bitcast.24, ...), custom_call_target="tpu_custom_call" | custom-call | tf_op jit(solution)/shard_map/operator/pallas_call | solution.py:248
  50.0 20.6 %image_gather.1.image_ref = bf16[16,3,16,1024]{3,2,1,0:T(8,128)(2,1)S(1)} custom-call(bf16[3,16,1024]{2,1,0:T(8,128)(2,1)S(1)} %operator.1.image_ref), custom_call_target="tpu_custom_call" | custom-call | tf_op jit(solution)/shard_map/image_gather/pallas_call | solution.py:317
  70.6 2.9 %synthesis.1 = f32[3,32,8192]{2,1,0:T(8,128)} custom-call(bf16[256,256]{1,0:T(8,128)(2,1)S(1)} %copy.25.hi_ref, bf16[256,256]{1,0:T(8,128)(2,1)S(1)} %copy.26.lo_ref, bf16[16,3,16,1024]{3,2,1,0:T(8,128)(2,1)S(1)} %image_gather.1.image_ref), custom_call_target="tpu_custom_call" | custom-call | tf_op jit(solution)/shard_map/synthesis/pallas_call | solution.py:348
  (12 shorter events, 0.1 us)
Async XLA Ops:
  0.0 17.8 %copy-start = (f32[32,3,8192]{2,0,1:T(8,128)S(1)}, f32[32,3,8192]{2,0,1:T(8,128)}, u32[]{:S(2)}) copy-start(f32[32,3,8192]{2,0,1:T(8,128)} %param.7) | copy-start | bytes 9437188
  16.6 19.2 %copy-start.1 = (bf16[1,64,2,32,3,128]{5,3,4,2,1,0:T(8,128)(2,1)S(1)}, bf16[1,64,2,32,3,128]{5,3,4,2,1,0:T(8,128)(2,1)}, u32[]{:S(2)}) copy-start(bf16[1,64,2,32,3,128]{5,3,4,2,1,0:T(8,128)(2,1)} %param.12) | copy-start | bytes 9437188
  35.8 1.9 %copy-start.2 = (bf16[1,64,2,32,3,128]{5,3,4,2,1,0:T(8,128)(2,1)S(1)}, bf16[1,64,2,32,3,128]{5,3,4,2,1,0:T(8,128)(2,1)}, u32[]{:S(2)}) copy-start(bf16[1,64,2,32,3,128]{5,3,4,2,1,0:T(8,128)(2,1)} %param.11) | copy-start | bytes 9437188
  37.7 1.6 %copy-start.3 = (bf16[1,64,8,2,1024]{4,3,2,1,0:T(2,128)(2,1)S(1)}, bf16[1,64,8,2,1024]{4,3,2,1,0:T(2,128)(2,1)}, u32[]{:S(2)}) copy-start(bf16[1,64,8,2,1024]{4,3,2,1,0:T(2,128)(2,1)} %param.13) | copy-start | bytes 6291460
where the time goes:
time: 74 us; the launch traced here: 73.6 us
  Pallas kernels  52.2 us (71%)
  local copies, waits for them, and re-layouts  13.9 us (19%)
  other arithmetic  7.28 us (10%)
    pallas_call x1, Pallas kernels, gather_images(): pl.pallas_call(functools.partial(gather_kernel, zs, ys), out_shape=jax.Sh...  20.6 us
    pallas_call x1, Pallas kernels, scatter_spectra(): pl.pallas_call(functools.partial(scatter_kernel, zs, ys), out_shape=jax.S...  18 us
    pallas_call x1, Pallas kernels, apply_operator(): pl.pallas_call(operator_kernel, out_shape=jax.ShapeDtypeStruct(spectrum.s...  10.7 us
    unnamed x10, local copies, waits for them, and re-layouts  4.77 us
    mul x4, local copies, waits for them, and re-layouts, inverse_matrix(): part[None, :, :, :, None] * eye[:, None, None, None, :]  4.63 us
    mul x2, local copies, waits for them, and re-layouts, forward_matrix(): part[:, :, None, None, :] * eye[None, None, :, :, None]  4.18 us
    pallas_call x1, Pallas kernels, synthesize(): pl.pallas_call(synthesis_kernel, grid=(3,), out_shape=jax.ShapeDtypeStruc...  2.92 us
    unnamed x1, other arithmetic  1.57 us

commit v1 on v0

--- a/solution.py
+++ b/solution.py
@@ -22,30 +22,46 @@
     return hi, lo
 
 
-def forward_matrix(frequency_ids, time_ids):
-    phases = frequency_ids[:, None] * time_ids[None, :] % STEPS
-    angles = phases.astype(jnp.float32) * (2.0 * math.pi / STEPS)
-    weights = DAMPING ** (time_ids.astype(jnp.float32) / STEPS)
-    table = jnp.stack([weights[None, :] * jnp.cos(angles), -weights[None, :] * jnp.sin(angles)], axis=1)
-    hi, lo = split_f32(table)
-    eye = jnp.eye(CHUNKS, dtype=jnp.bfloat16)
-    rows = table.shape[0] * 2 * CHUNKS
-    spread = lambda part: (part[:, :, None, None, :] * eye[None, None, :, :, None]).reshape(rows, -1)
-    return jnp.concatenate([spread(hi), spread(hi), spread(lo)], axis=1)
-
-
-def inverse_matrix(frequency_ids, time_ids):
-    phases = time_ids[:, None] * frequency_ids[None, :] % STEPS
-    angles = phases.astype(jnp.float32) * (2.0 * math.pi / STEPS)
-    scales = DAMPING ** (-time_ids.astype(jnp.float32) / STEPS) / STEPS
-    doubled = jnp.where((frequency_ids == 0) | (frequency_ids == STEPS // 2), 1.0, 2.0)
-    factor = scales[:, None] * doubled[None, :]
-    table = jnp.stack([factor * jnp.cos(angles), -factor * jnp.sin(angles)], axis=2)
-    hi, lo = split_f32(table)
-    eye = jnp.eye(CHUNKS, dtype=jnp.bfloat16)
-    rows = table.shape[0] * CHUNKS
-    spread = lambda part: (part[None, :, :, :, None] * eye[:, None, None, None, :]).reshape(rows, -1)
-    return spread(hi), spread(lo)
+def iota(shape, axis):
+    return lax.broadcasted_iota(jnp.int32, shape, axis)
+
+
+def angles_of(frequencies, times):
+    phases = (frequencies * times) & (STEPS - 1)
+    return phases.astype(jnp.float32) * (2.0 * math.pi / STEPS)
+
+
+def forward_matrix(ids, first_time, times):
+    n = ids.shape[1]
+    lanes, rows = CHUNKS * times, n * 2 * CHUNKS
+    column = jnp.sum(jnp.where(iota((n, n), 0) == iota((n, n), 1), ids, 0), axis=1, keepdims=True)
+    time_ids = iota((n, lanes), 1) % times + first_time
+    angles = angles_of(column, time_ids)
+    weights = jnp.exp2(time_ids.astype(jnp.float32) * (math.log2(DAMPING) / STEPS))
+    table = jnp.concatenate([weights * jnp.cos(angles), -weights * jnp.sin(angles)], axis=0)
+    row = iota((rows, 2 * n), 0)
+    spread = (iota((rows, 2 * n), 1) == (row // CHUNKS) % 2 * n + row // (2 * CHUNKS)).astype(jnp.bfloat16)
+    kept = iota((rows, lanes), 0) % CHUNKS == iota((rows, lanes), 1) // times
+    hi, lo = [
+        jnp.where(kept, jnp.dot(spread, part, preferred_element_type=jnp.float32), 0.0).astype(jnp.bfloat16)
+        for part in split_f32(table)]
+    return hi, lo
+
+
+def inverse_matrix(ids, first_time, times):
+    n = ids.shape[1]
+    rows, lanes = CHUNKS * times, n * 2 * CHUNKS
+    time_ids = iota((rows, n), 0) % times + first_time
+    angles = angles_of(ids, time_ids)
+    scales = jnp.exp2(time_ids.astype(jnp.float32) * (-math.log2(DAMPING) / STEPS)) / STEPS
+    factor = scales * jnp.where((ids == 0) | (ids == STEPS // 2), 1.0, 2.0)
+    table = jnp.concatenate([factor * jnp.cos(angles), -factor * jnp.sin(angles)], axis=1)
+    lane = iota((2 * n, lanes), 1)
+    spread = (iota((2 * n, lanes), 0) == (lane // CHUNKS) % 2 * n + lane // (2 * CHUNKS)).astype(jnp.bfloat16)
+    kept = iota((rows, lanes), 1) % CHUNKS == iota((rows, lanes), 0) // times
+    return [
+        jnp.where(kept, jnp.dot(part, spread, preferred_element_type=jnp.float32), 0.0).astype(jnp.bfloat16)
+        for part in split_f32(table)]
 
 
 def place(zs, ys):
@@ -74,18 +90,20 @@
     return targets
 
 
-def scatter_kernel(zs, ys, table_ref, slip_ref, out_ref, acc, send0, recv0, send1, recv1, send2, recv2, *sems):
+def scatter_kernel(zs, ys, ids_ref, slip_ref, out_ref, acc, send0, recv0, send1, recv1, send2, recv2, *sems):
     ss0, rs0, ss1, rs1, ss2, rs2 = sems
     z, y, core = place(zs, ys)
     ready = greet(partners(z, y, core, zs, ys))
     times, width = slip_ref.shape[1], slip_ref.shape[2] // CHUNKS
     order = list(range(zs // 2, zs // 2 - zs, -1))
     order = [s % zs for s in order if s % zs] + [0]
+    table_hi, table_lo = forward_matrix(ids_ref[...], index_of(z, y, core, ys) * times, times)
+    table = jnp.concatenate([table_hi, table_hi, table_lo], axis=1)
     for j in range(3):
         x = jnp.concatenate([slip_ref[j, :, c * width:(c + 1) * width] for c in range(CHUNKS)], axis=0)
         hi, lo = split_f32(x)
         stack = jnp.concatenate([hi, lo, hi], axis=0)
-        res = jnp.dot(table_ref[...], stack, preferred_element_type=jnp.float32)
+        res = jnp.dot(table, stack, preferred_element_type=jnp.float32)
         res = res.reshape(zs * ys, 2, 2 * CHUNKS, width)
         first, second = res[:, 0], res[:, 1]
         own = jnp.where(core == 0, first, second)
@@ -130,19 +148,19 @@
     for s in order[:-1]:
         stage2[s].wait_recv()
         total += recv2[s - 1].astype(jnp.float32)
-    out_ref[...] = total.astype(jnp.bfloat16)
+    out_ref[...] = total
     for copies in (stage0, stage1, stage2):
         for copy in copies.values():
             copy.wait_send()
 
 
-def scatter_spectra(table, slip, zs, ys):
+def scatter_spectra(ids, slip, zs, ys):
     block = (3, 2 * CHUNKS, slip.shape[2] // CHUNKS)
     bf16 = jnp.bfloat16
     high, many = max(ys - 1, 1), max(zs - 1, 1)
     return pl.pallas_call(
         functools.partial(scatter_kernel, zs, ys),
-        out_shape=jax.ShapeDtypeStruct(block, bf16),
+        out_shape=jax.ShapeDtypeStruct(block, jnp.float32),
         in_specs=[pl.BlockSpec(memory_space=pltpu.VMEM)] * 2,
         out_specs=pl.BlockSpec(memory_space=pltpu.VMEM),
         scratch_shapes=[
@@ -160,9 +178,9 @@
             pltpu.SemaphoreType.DMA((many,)),
             pltpu.SemaphoreType.DMA((many,)),
         ],
-        compiler_params=pltpu.CompilerParams(collective_id=0, has_side_effects=True, vmem_limit_bytes=48 * MIB),
+        compiler_params=pltpu.CompilerParams(collective_id=0, has_side_effects=True, vmem_limit_bytes=(12 + zs * ys * 5 // 4) * MIB),
         name="spectra_scatter",
-    )(table, slip)
+    )(ids, slip)
 
 
 def operator_kernel(spec_ref, right_ref, coupling_ref, left_ref, rank_ref, col_ref, image_ref, coef, tiled, sums):
@@ -176,25 +194,30 @@
     for g in range(groups):
         lanes = slice(g * LEAF, (g + 1) * LEAF)
         x = jnp.concatenate([spec_ref[j, :, lanes] for j in range(3)], axis=1)
+        x = jnp.concatenate(split_f32(x), axis=0)
         prod = jnp.zeros((2 * CHUNKS, 2 * rank), f32)
         for h in range(2):
             basis = jnp.concatenate(
                 [jnp.concatenate([right_ref[(h * half + c) * groups + g, q, j] for c in range(half) for q in range(2)], axis=0)
                  for j in range(3)], axis=1)
             full = lax.dot_general(x, basis, (((1,), (1,)), ((), ())), preferred_element_type=f32)
+            full = full[:2 * CHUNKS] + full[2 * CHUNKS:]
             for c in range(half):
                 prod = jnp.where(chunk_row == h * half + c, full[:, c * 2 * rank:(c + 1) * 2 * rank], prod)
         low, high = prod[:CHUNKS], prod[CHUNKS:]
         rows = slice(g * CHUNKS, (g + 1) * CHUNKS)
         coef[0, rows] = low[:, :rank] - high[:, rank:]
         coef[1, rows] = high[:, :rank] + low[:, rank:]
-    kept = lax.broadcasted_iota(jnp.int32, (clusters, rank), 1) < rank_ref[...]
+    square = (clusters, clusters)
+    cluster_of = iota(square, 0) % CHUNKS * groups + iota(square, 0) // CHUNKS
+    ranks = jnp.sum(jnp.where(iota(square, 1) == cluster_of, rank_ref[...], 0), axis=1, keepdims=True)
+    kept = iota((clusters, rank), 1) < ranks
     area = rank * rank
     lane_of = lax.broadcasted_iota(jnp.int32, (rank, area), 1)
     spread = (lane_of % rank == lax.broadcasted_iota(jnp.int32, (rank, area), 0)).astype(bf16)
     for p in range(2):
-        held = jnp.where(kept, coef[p], 0.0).astype(bf16)
-        tiled[p] = jnp.dot(held, spread, preferred_element_type=f32)
+        hi, lo = split_f32(jnp.where(kept, coef[p], 0.0))
+        tiled[p] = jnp.dot(hi, spread, preferred_element_type=f32) + jnp.dot(lo, spread, preferred_element_type=f32)
 
     def couple(step, carry):
         found = [[], []]
@@ -202,7 +225,7 @@
             a = step * 4 + r
             totals = [jnp.zeros((2, area), f32), jnp.zeros((2, area), f32)]
             for i in range(blocks):
-                source = col_ref[a, i]
+                source = col_ref[i, a]
                 row = (source % groups) * CHUNKS + source // groups
                 block = coupling_ref[a, i].astype(f32)
                 for p in range(2):
@@ -233,17 +256,17 @@
         mixed = jnp.concatenate([
             jnp.concatenate([real[rows], -imag[rows]], axis=1),
             jnp.concatenate([imag[rows], real[rows]], axis=1)], axis=0)
-        masked = jnp.concatenate([jnp.where(chunk_row == c, mixed, 0.0) for c in range(CHUNKS)], axis=1).astype(bf16)
+        masked = jnp.concatenate([jnp.where(chunk_row == c, mixed, 0.0) for c in range(CHUNKS)], axis=1)
+        masked = jnp.concatenate(split_f32(masked), axis=0)
         for j in range(3):
             basis = jnp.concatenate([left_ref[c * groups + g, q, j] for c in range(CHUNKS) for q in range(2)], axis=0)
             out = jnp.dot(masked, basis, preferred_element_type=f32)
+            out = out[:2 * CHUNKS] + out[2 * CHUNKS:]
             image_ref[j, :, g * LEAF:(g + 1) * LEAF] = out.astype(bf16)
 
 
 def apply_operator(spectrum, right, coupling, left, ranks, col_clusters):
     clusters, rank = right.shape[0], right.shape[3]
-    groups = clusters // CHUNKS
-    order = ranks.reshape(CHUNKS, groups).T.reshape(clusters, 1)
     vmem = pl.BlockSpec(memory_space=pltpu.VMEM)
     return pl.pallas_call(
         operator_kernel,
@@ -255,12 +278,12 @@
             pltpu.VMEM((2, clusters, rank * rank), jnp.float32),
             pltpu.VMEM((2, 2 * clusters, rank * rank), jnp.float32),
         ],
-        compiler_params=pltpu.CompilerParams(vmem_limit_bytes=40 * MIB),
+        compiler_params=pltpu.CompilerParams(vmem_limit_bytes=24 * MIB),
         name="operator",
-    )(spectrum, right, coupling, left, order, col_clusters)
-
-
-def gather_kernel(zs, ys, image_ref, out_ref, local_sem, *sems):
+    )(spectrum, right, coupling, left, ranks, col_clusters.T)
+
+
+def gather_kernel(zs, ys, times, image_ref, ids_ref, out_ref, hi_ref, lo_ref, local_sem, *sems):
     zsend, zrecv, ysend, yrecv, csend, crecv = sems
     z, y, core = place(zs, ys)
     ready = greet(partners(z, y, core, zs, ys))
@@ -270,67 +293,77 @@
     ready()
     copies = []
 
-    def send(block, source, target, send_sem, recv_sem):
+    def send(block, j, source, target, send_sem, recv_sem):
         copy = pltpu.make_async_remote_copy(
-            src_ref=source, dst_ref=out_ref.at[block], send_sem=send_sem, recv_sem=recv_sem,
+            src_ref=source.at[j], dst_ref=out_ref.at[block, j], send_sem=send_sem, recv_sem=recv_sem,
             device_id={"freq": target}, device_id_type=MESH)
         copy.start()
         copies.append(copy)
-        return copy
 
     other = index_of(z, y, 1 - core, ys)
-    order = [s % zs for s in range(zs // 2, zs // 2 - zs, -1) if s % zs]
-    for s in order:
-        send(me, image_ref, index_of(lax.rem(z + s, zs), y, core, ys), zsend.at[s - 1], zrecv.at[s - 1])
-    for step in range(1, ys):
-        send(me, image_ref, index_of(z, lax.rem(y + step, ys), core, ys), ysend.at[step - 1, 0], yrecv.at[step - 1, 0])
-    send(me, image_ref, other, csend.at[0, 0], crecv.at[0, 0])
-
-    def arrived(block, recv_sem):
-        pltpu.make_async_copy(out_ref.at[block], out_ref.at[block], recv_sem).wait()
-
-    near = sorted(range(1, zs), key=lambda s: min(s, zs - s))
-    for s in near:
-        block = index_of(lax.rem(z + zs - s, zs), y, core, ys)
-        arrived(block, zrecv.at[s - 1])
+    far = sorted(range(1, zs), key=lambda s: -min(s, zs - s))
+    near = far[::-1]
+
+    def pass_y(block, j, source, s):
         for step in range(1, ys):
-            send(block, out_ref.at[block], index_of(z, lax.rem(y + step, ys), core, ys),
-                 ysend.at[step - 1, s], yrecv.at[step - 1, s])
-        send(block, out_ref.at[block], other, csend.at[0, s], crecv.at[0, s])
-    for s in [0] + near:
-        for step in range(1, ys):
-            block = index_of(lax.rem(z + zs - s, zs), lax.rem(y + ys - step, ys), core, ys)
-            arrived(block, yrecv.at[step - 1, s])
-            send(block, out_ref.at[block], other, csend.at[step, s], crecv.at[step, s])
-    for s in [0] + near:
-        for step in range(ys):
-            block = index_of(lax.rem(z + zs - s, zs), lax.rem(y + ys - step, ys), 1 - core, ys)
-            arrived(block, crecv.at[step, s])
+            send(block, j, source, index_of(z, lax.rem(y + step, ys), core, ys),
+                 ysend.at[step - 1, s, j], yrecv.at[step - 1, s, j])
+
+    def arrived(block, j, recv_sem):
+        pltpu.make_async_copy(out_ref.at[block, j], out_ref.at[block, j], recv_sem).wait()
+
+    pieces = range(3)
+    for j in pieces:
+        for s in far:
+            send(me, j, image_ref, index_of(lax.rem(z + s, zs), y, core, ys), zsend.at[s - 1, j], zrecv.at[s - 1, j])
+        pass_y(me, j, image_ref, 0)
+        send(me, j, image_ref, other, csend.at[0, 0, j], crecv.at[0, 0, j])
+    hi_ref[...], lo_ref[...] = inverse_matrix(ids_ref[...], me * times, times)
+
+    for j in pieces:
+        for s in near:
+            block = index_of(lax.rem(z + zs - s, zs), y, core, ys)
+            arrived(block, j, zrecv.at[s - 1, j])
+            pass_y(block, j, out_ref.at[block], s)
+            send(block, j, out_ref.at[block], other, csend.at[0, s, j], crecv.at[0, s, j])
+    for j in pieces:
+        for s in [0] + near:
+            for step in range(1, ys):
+                block = index_of(lax.rem(z + zs - s, zs), lax.rem(y + ys - step, ys), core, ys)
+                arrived(block, j, yrecv.at[step - 1, s, j])
+                send(block, j, out_ref.at[block], other, csend.at[step, s, j], crecv.at[step, s, j])
+    for j in pieces:
+        for s in [0] + near:
+            for step in range(ys):
+                block = index_of(lax.rem(z + zs - s, zs), lax.rem(y + ys - step, ys), 1 - core, ys)
+                arrived(block, j, crecv.at[step, s, j])
     mine.wait()
     for copy in copies:
         copy.wait_send()
 
 
-def gather_images(image, zs, ys):
+def gather_images(image, ids, times, zs, ys):
     high, many = max(ys - 1, 1), max(zs - 1, 1)
+    n = zs * ys * 2
     vmem = pl.BlockSpec(memory_space=pltpu.VMEM)
+    matrix = jax.ShapeDtypeStruct((CHUNKS * times, n * 2 * CHUNKS), jnp.bfloat16)
     return pl.pallas_call(
-        functools.partial(gather_kernel, zs, ys),
-        out_shape=jax.ShapeDtypeStruct((zs * ys * 2,) + image.shape, image.dtype),
-        in_specs=[vmem],
-        out_specs=vmem,
+        functools.partial(gather_kernel, zs, ys, times),
+        out_shape=(jax.ShapeDtypeStruct((n,) + image.shape, image.dtype), matrix, matrix),
+        in_specs=[vmem, vmem],
+        out_specs=(vmem, vmem, vmem),
         scratch_shapes=[
             pltpu.SemaphoreType.DMA,
-            pltpu.SemaphoreType.DMA((many,)),
-            pltpu.SemaphoreType.DMA((many,)),
-            pltpu.SemaphoreType.DMA((high, zs)),
-            pltpu.SemaphoreType.DMA((high, zs)),
-            pltpu.SemaphoreType.DMA((ys, zs)),
-            pltpu.SemaphoreType.DMA((ys, zs)),
+            pltpu.SemaphoreType.DMA((many, 3)),
+            pltpu.SemaphoreType.DMA((many, 3)),
+            pltpu.SemaphoreType.DMA((high, zs, 3)),
+            pltpu.SemaphoreType.DMA((high, zs, 3)),
+            pltpu.SemaphoreType.DMA((ys, zs, 3)),
+            pltpu.SemaphoreType.DMA((ys, zs, 3)),
         ],
-        compiler_params=pltpu.CompilerParams(collective_id=1, has_side_effects=True, vmem_limit_bytes=32 * MIB),
+        compiler_params=pltpu.CompilerParams(collective_id=1, has_side_effects=True, vmem_limit_bytes=24 * MIB),
         name="image_gather",
-    )(image)
+    )(image, ids)
 
 
 def synthesis_kernel(hi_ref, lo_ref, image_ref, out_ref):
@@ -358,14 +391,13 @@
 
 def body(zs, ys, slip_history, frequency_ids, col_clusters, basis_ranks, left_basis, right_basis, coupling):
     times = slip_history.shape[0]
-    time_ids = lax.axis_index("freq") * times + jnp.arange(times, dtype=jnp.int32)
+    ids = frequency_ids.reshape(1, -1)
     slip = jnp.transpose(slip_history, (1, 0, 2))
     right = jnp.transpose(right_basis[0], (0, 1, 3, 2, 4))
     left = jnp.transpose(left_basis[0], (0, 1, 3, 2, 4))
-    spectrum = scatter_spectra(forward_matrix(frequency_ids, time_ids), slip, zs, ys)
-    image = apply_operator(spectrum, right, coupling[0], left, basis_ranks[0], col_clusters)
-    images = gather_images(image, zs, ys)
-    hi, lo = inverse_matrix(frequency_ids, time_ids)
+    spectrum = scatter_spectra(ids, slip, zs, ys)
+    image = apply_operator(spectrum, right, coupling[0], left, basis_ranks, col_clusters)
+    images, hi, lo = gather_images(image, ids, times, zs, ys)
     traction = synthesize(hi, lo, images, times)
     return jnp.transpose(traction, (1, 0, 2))
 

time: 74 us -> 57.3 us (0.77)
  the two profiles are of different devices: /device:TPU:21 before, /device:TPU:9 now
where the time goes in v1:
time: 57.3 us; the launch traced here: 56.8 us
  Pallas kernels  50.7 us (88%)
  local copies, waits for them, and re-layouts  6.06 us (11%)
    pallas_call x1, Pallas kernels, scatter_spectra(): pl.pallas_call(functools.partial(scatter_kernel, zs, ys), out_shape=jax.S...  18.6 us
    pallas_call x1, Pallas kernels, gather_images(): pl.pallas_call(functools.partial(gather_kernel, zs, ys, times), out_shape...  18.4 us
    pallas_call x1, Pallas kernels, apply_operator(): pl.pallas_call(operator_kernel, out_shape=jax.ShapeDtypeStruct(spectrum.s...  10.7 us
    unnamed x16, local copies, waits for them, and re-layouts  6.06 us
    pallas_call x1, Pallas kernels, synthesize(): pl.pallas_call(synthesis_kernel, grid=(3,), out_shape=jax.ShapeDtypeStruc...  2.92 us

profile of v1, /device:TPU:9, one launch (start us, length us, event | category | flops | bytes accessed | tf_op | source)
XLA Modules:
  0.0 56.8 jit_solution(523331567369701022)
XLA Ops:
  0.0 0.0 copy-start.7
  0.0 0.0 copy-start.4
  0.0 0.0 copy-start
  0.0 1.9 %copy-done = f32[32,3,8192]{2,0,1:T(8,128)S(1)} copy-done((f32[32,3,8192]{2,0,1:T(8,128)S(1)}, f32[32,3,8192]{2,0,1:T(8,128)}, u32[]{:S(2)}) %copy-start) | copy-done | bytes 3145752
  1.9 0.0 copy-start.5
  1.9 0.7 %copy-done.5 = s32[16]{0:T(128)S(1)} copy-done((s32[16]{0:T(128)S(1)}, s32[16]{0:T(128)}, u32[]{:S(2)}) %copy-start.5) | copy-done | bytes 88
  2.6 0.0 copy-start.1
  2.6 18.6 %spectra_scatter.1.spec_ref = f32[3,16,1024]{2,1,0:T(8,128)S(1)} custom-call(s32[1,16]{1,0:T(1,128)S(1)} %bitcast.16, f32[3,32,8192]{2,1,0:T(8,128)S(1)} %bitcast.11), custom_call_target="tpu_custom_call" | custom-call | tf_op jit(solution)/shard_map/spectra_scatter/pallas_call | solution.py:161
  21.2 0.0 copy-done.7
  21.2 0.0 copy-done.4
  21.2 0.0 copy-done.1
  21.2 0.0 copy-start.2
  21.2 1.9 %copy-done.2 = bf16[1,64,2,32,3,128]{5,3,4,2,1,0:T(8,128)(2,1)S(1)} copy-done((bf16[1,64,2,32,3,128]{5,3,4,2,1,0:T(8,128)(2,1)S(1)}, bf16[1,64,2,32,3,128]{5,3,4,2,1,0:T(8,128)(2,1)}, u32[]{:S(2)}) %copy-start.2) | copy-done | bytes 3145752
  23.1 0.0 copy-start.3
  23.1 1.6 %copy-done.3 = bf16[1,64,8,2,1024]{4,3,2,1,0:T(2,128)(2,1)S(1)} copy-done((bf16[1,64,8,2,1024]{4,3,2,1,0:T(2,128)(2,1)S(1)}, bf16[1,64,8,2,1024]{4,3,2,1,0:T(2,128)(2,1)}, u32[]{:S(2)}) %copy-start.3) | copy-done | bytes 2097176
  24.7 0.0 copy-start.6
  24.7 10.7 %operator.1.image_ref = bf16[3,16,1024]{2,1,0:T(8,128)(2,1)S(1)} custom-call(f32[3,16,1024]{2,1,0:T(8,128)S(1)} %spectra_scatter.1.spec_ref, bf16[64,2,3,32,128]{4,3,2,1,0:T(8,128)(2,1)S(1)} %bitcast.12, bf16[64,8,2,1024]{3,2,1,0:T(2,128)(2,1)S(1)} %bitcast.14, bf16[64,2,3,32,128]{4,3,2,1,0:T(8,128)(2,1)S(1)} %bitcast.13, s32[1,64]{1,0:T(1,128)S(1)} %copy-done.7, ...), custom_call_target="tpu_custom_call" | custom-call | tf_op jit(solution)/shard_map/operator/pallas_call | solution.py:271
  35.5 0.0 copy-done.6
  35.5 18.4 %image_gather.1 = (bf16[16,3,16,1024]{3,2,1,0:T(8,128)(2,1)S(1)}, bf16[256,256]{1,0:T(8,128)(2,1)S(1)}, bf16[256,256]{1,0:T(8,128)(2,1)S(1)}) custom-call(bf16[3,16,1024]{2,1,0:T(8,128)(2,1)S(1)} %operator.1.image_ref, s32[1,16]{1,0:T(1,128)S(1)} %bitcast.17), custom_call_target="tpu_custom_call" | custom-call | tf_op jit(solution)/shard_map/image_gather/pallas_call | solution.py:350
  53.9 2.9 %synthesis.1 = f32[3,32,8192]{2,1,0:T(8,128)} custom-call(bf16[256,256]{1,0:T(8,128)(2,1)S(1)} %get-tuple-element.8.hi_ref, bf16[256,256]{1,0:T(8,128)(2,1)S(1)} %get-tuple-element.9.lo_ref, bf16[16,3,16,1024]{3,2,1,0:T(8,128)(2,1)S(1)} %get-tuple-element.10.image_ref), custom_call_target="tpu_custom_call" | custom-call | tf_op jit(solution)/shard_map/synthesis/pallas_call | solution.py:381
Async XLA Ops:
  0.0 21.2 %copy-start.7 = (s32[1,64]{1,0:T(1,128)S(1)}, s32[1,64]{1,0:T(1,128)}, u32[]{:S(2)}) copy-start(s32[1,64]{1,0:T(1,128)} %rank_ref.1) | copy-start | bytes 772
  0.0 21.2 %copy-start.4 = (s32[64,8]{0,1:T(8,128)S(1)}, s32[64,8]{0,1:T(8,128)}, u32[]{:S(2)}) copy-start(s32[64,8]{0,1:T(8,128)} %param.9) | copy-start | bytes 6148
  0.0 1.9 %copy-start = (f32[32,3,8192]{2,0,1:T(8,128)S(1)}, f32[32,3,8192]{2,0,1:T(8,128)}, u32[]{:S(2)}) copy-start(f32[32,3,8192]{2,0,1:T(8,128)} %param.7) | copy-start | bytes 9437188
  1.9 0.7 %copy-start.5 = (s32[16]{0:T(128)S(1)}, s32[16]{0:T(128)}, u32[]{:S(2)}) copy-start(s32[16]{0:T(128)} %param.8) | copy-start | bytes 196
  2.6 18.6 %copy-start.1 = (bf16[1,64,2,32,3,128]{5,3,4,2,1,0:T(8,128)(2,1)S(1)}, bf16[1,64,2,32,3,128]{5,3,4,2,1,0:T(8,128)(2,1)}, u32[]{:S(2)}) copy-start(bf16[1,64,2,32,3,128]{5,3,4,2,1,0:T(8,128)(2,1)} %param.12) | copy-start | bytes 9437188
  21.2 1.9 %copy-start.2 = (bf16[1,64,2,32,3,128]{5,3,4,2,1,0:T(8,128)(2,1)S(1)}, bf16[1,64,2,32,3,128]{5,3,4,2,1,0:T(8,128)(2,1)}, u32[]{:S(2)}) copy-start(bf16[1,64,2,32,3,128]{5,3,4,2,1,0:T(8,128)(2,1)} %param.11) | copy-start | bytes 9437188
  23.1 1.6 %copy-start.3 = (bf16[1,64,8,2,1024]{4,3,2,1,0:T(2,128)(2,1)S(1)}, bf16[1,64,8,2,1024]{4,3,2,1,0:T(2,128)(2,1)}, u32[]{:S(2)}) copy-start(bf16[1,64,8,2,1024]{4,3,2,1,0:T(2,128)(2,1)} %param.13) | copy-start | bytes 6291460
  24.7 10.8 %copy-start.6 = (s32[16]{0:T(128)S(1)}, s32[16]{0:T(128)}, u32[]{:S(2)}) copy-start(s32[16]{0:T(128)} %param.8) | copy-start | bytes 196

commit v2 on v1

v2 whole, which is shorter than its diff:
```python
import functools
import math

import jax
import jax.numpy as jnp
from jax import lax
from jax.experimental import pallas as pl
from jax.experimental.pallas import tpu as pltpu
from jax.sharding import PartitionSpec as P

STEPS = 512
DAMPING = 0.5
LEAF = 128
CHUNKS = 8
MESH = pl.DeviceIdType.MESH
MIB = 1024 * 1024


def split_f32(x):
    hi = x.astype(jnp.bfloat16)
    lo = (x - hi.astype(jnp.float32)).astype(jnp.bfloat16)
    return hi, lo


def iota(shape, axis):
    return lax.broadcasted_iota(jnp.int32, shape, axis)


def angles_of(frequencies, times):
    phases = (frequencies * times) & (STEPS - 1)
    return phases.astype(jnp.float32) * (2.0 * math.pi / STEPS)


def forward_matrix(ids, first_time, times):
    n = ids.shape[1]
    lanes, rows = CHUNKS * times, n * 2 * CHUNKS
    column = jnp.sum(jnp.where(iota((n, n), 0) == iota((n, n), 1), ids, 0), axis=1, keepdims=True)
    time_ids = iota((n, lanes), 1) % times + first_time
    angles = angles_of(column, time_ids)
    weights = jnp.exp2(time_ids.astype(jnp.float32) * (math.log2(DAMPING) / STEPS))
    table = jnp.concatenate([weights * jnp.cos(angles), -weights * jnp.sin(angles)], axis=0)
    row = iota((rows, 2 * n), 0)
    spread = (iota((rows, 2 * n), 1) == (row // CHUNKS) % 2 * n + row // (2 * CHUNKS)).astype(jnp.bfloat16)
    kept = iota((rows, lanes), 0) % CHUNKS == iota((rows, lanes), 1) // times
    hi, lo = [
        jnp.where(kept, jnp.dot(spread, part, preferred_element_type=jnp.float32), 0.0).astype(jnp.bfloat16)
        for part in split_f32(table)]
    return hi, lo


def inverse_matrix(ids, first_time, times):
    n = ids.shape[1]
    rows, lanes = CHUNKS * times, n * 2 * CHUNKS
    time_ids = iota((rows, n), 0) % times + first_time
    angles = angles_of(ids, time_ids)
    scales = jnp.exp2(time_ids.astype(jnp.float32) * (-math.log2(DAMPING) / STEPS)) / STEPS
    factor = scales * jnp.where((ids == 0) | (ids == STEPS // 2), 1.0, 2.0)
    table = jnp.concatenate([factor * jnp.cos(angles), -factor * jnp.sin(angles)], axis=1)
    lane = iota((2 * n, lanes), 1)
    spread = (iota((2 * n, lanes), 0) == (lane // CHUNKS) % 2 * n + lane // (2 * CHUNKS)).astype(jnp.bfloat16)
    kept = iota((rows, lanes), 1) % CHUNKS == iota((rows, lanes), 0) // times
    return [
        jnp.where(kept, jnp.dot(part, spread, preferred_element_type=jnp.float32), 0.0).astype(jnp.bfloat16)
        for part in split_f32(table)]


def place(zs, ys):
    me = lax.axis_index("freq")
    core = lax.rem(me, 2)
    y = lax.rem(me // 2, ys)
    z = me // (2 * ys)
    return z, y, core


def index_of(z, y, core, ys):
    return (z * ys + y) * 2 + core


def greet(targets):
    barrier = pltpu.get_barrier_semaphore()
    for target in targets:
        pl.semaphore_signal(barrier, inc=1, device_id={"freq": target}, device_id_type=MESH)
    return lambda: pl.semaphore_wait(barrier, len(targets))


def partners(z, y, core, zs, ys):
    targets = [index_of(z, y, 1 - core, ys)]
    targets += [index_of(z, lax.rem(y + s, ys), core, ys) for s in range(1, ys)]
    targets += [index_of(lax.rem(z + s, zs), y, core, ys) for s in range(1, zs)]
    return targets


def scatter_phase(zs, ys, ready, ids, slip_ref, slip_sems, between, acc, send0, recv0, send1, recv1, send2, recv2, sems):
    ss0, rs0, ss1, rs1, ss2, rs2 = sems
    z, y, core = place(zs, ys)
    times, width = slip_ref.shape[1], slip_ref.shape[2] // CHUNKS
    order = list(range(zs // 2, zs // 2 - zs, -1))
    order = [s % zs for s in order if s % zs] + [0]
    table_hi, table_lo = forward_matrix(ids, index_of(z, y, core, ys) * times, times)
    table = jnp.concatenate([table_hi, table_hi, table_lo], axis=1)
    for j in range(3):
        pltpu.make_async_copy(slip_ref.at[j], slip_ref.at[j], slip_sems.at[j]).wait()
        x = jnp.concatenate([slip_ref[j, :, c * width:(c + 1) * width] for c in range(CHUNKS)], axis=0)
        hi, lo = split_f32(x)
        stack = jnp.concatenate([hi, lo, hi], axis=0)
        res = jnp.dot(table, stack, preferred_element_type=jnp.float32)
        res = res.reshape(zs * ys, 2, 2 * CHUNKS, width)
        first, second = res[:, 0], res[:, 1]
        own = jnp.where(core == 0, first, second)
        other = jnp.where(core == 0, second, first)
        acc[:, j] = own
        send0[:, j] = other.astype(jnp.bfloat16)
    ready()
    stage0 = {}
    for s in order:
        at = lax.rem(z + s, zs)
        rows = pl.ds(at * ys, ys)
        stage0[s] = pltpu.make_async_remote_copy(
            src_ref=send0.at[rows], dst_ref=recv0.at[rows], send_sem=ss0.at[s], recv_sem=rs0.at[s],
            device_id={"freq": index_of(z, y, 1 - core, ys)}, device_id_type=MESH)
        stage0[s].start()
    stage1, stage2 = {}, {}
    for s in order:
        at = lax.rem(z + s, zs)
        stage0[s].wait_recv()
        for step in range(1, ys):
            there = lax.rem(y + step, ys)
            block = at * ys + there
            send1[step - 1, at] = (acc[block] + recv0[block].astype(jnp.float32)).astype(jnp.bfloat16)
            stage1[s, step] = pltpu.make_async_remote_copy(
                src_ref=send1.at[step - 1, at], dst_ref=recv1.at[step - 1, at],
                send_sem=ss1.at[step - 1, s], recv_sem=rs1.at[step - 1, s],
                device_id={"freq": index_of(z, there, core, ys)}, device_id_type=MESH)
            stage1[s, step].start()
    between()
    for s in order:
        at = lax.rem(z + s, zs)
        block = at * ys + y
        total = acc[block] + recv0[block].astype(jnp.float32)
        for step in range(1, ys):
            stage1[s, step].wait_recv()
            total += recv1[step - 1, at].astype(jnp.float32)
        if s:
            send2[s - 1] = total.astype(jnp.bfloat16)
            stage2[s] = pltpu.make_async_remote_copy(
                src_ref=send2.at[s - 1], dst_ref=recv2.at[s - 1], send_sem=ss2.at[s - 1], recv_sem=rs2.at[s - 1],
                device_id={"freq": index_of(at, y, core, ys)}, device_id_type=MESH)
            stage2[s].start()
    for s in order[:-1]:
        stage2[s].wait_recv()
        total += recv2[s - 1].astype(jnp.float32)
    for copies in (stage0, stage1, stage2):
        for copy in copies.values():
            copy.wait_send()
    return total


def reorder_coupling(coupling_ref, ordered):
    groups, blocks = coupling_ref.shape[0] // CHUNKS, coupling_ref.shape[1]

    def step(g, carry):
        rows = pl.ds(pl.multiple_of(g * CHUNKS, CHUNKS), CHUNKS)
        for i in range(blocks):
            found = [coupling_ref[c * groups + g, i].astype(jnp.float32) for c in range(CHUNKS)]
            for q in range(2):
                ordered[q, i, rows, :] = jnp.concatenate([part[q:q + 1] for part in found], axis=0)
        return carry

    lax.fori_loop(0, groups, step, 0)


def operator_phase(spectrum, right_ref, ordered, left_ref, wait_left, rank_row, col_ref, image_ref, coef):
    f32, bf16 = jnp.float32, jnp.bfloat16
    groups = spectrum.shape[2] // LEAF
    rank = right_ref.shape[3]
    clusters = groups * CHUNKS
    blocks = ordered.shape[1]
    chunk_row = lax.broadcasted_iota(jnp.int32, (2 * CHUNKS, 2 * rank), 0) % CHUNKS
    half = CHUNKS // 2
    for g in range(groups):
        lanes = slice(g * LEAF, (g + 1) * LEAF)
        x = jnp.concatenate([spectrum[j, :, lanes] for j in range(3)], axis=1)
        x = jnp.concatenate(split_f32(x), axis=0)
        prod = jnp.zeros((2 * CHUNKS, 2 * rank), f32)
        for h in range(2):
            basis = jnp.concatenate(
                [jnp.concatenate([right_ref[(h * half + c) * groups + g, q, j] for c in range(half) for q in range(2)], axis=0)
                 for j in range(3)], axis=1)
            full = lax.dot_general(x, basis, (((1,), (1,)), ((), ())), preferred_element_type=f32)
            full = full[:2 * CHUNKS] + full[2 * CHUNKS:]
            for c in range(half):
                prod = jnp.where(chunk_row == h * half + c, full[:, c * 2 * rank:(c + 1) * 2 * rank], prod)
        low, high = prod[:CHUNKS], prod[CHUNKS:]
        rows = slice(g * CHUNKS, (g + 1) * CHUNKS)
        coef[0, rows] = low[:, :rank] - high[:, rank:]
        coef[1, rows] = high[:, :rank] + low[:, rank:]
    square = (clusters, clusters)
    cluster_of = iota(square, 0) % CHUNKS * groups + iota(square, 0) // CHUNKS
    ranks = jnp.sum(jnp.where(iota(square, 1) == cluster_of, rank_row, 0), axis=1, keepdims=True)
    kept = iota((clusters, rank), 1) < ranks
    area = rank * rank
    spread = (iota((2 * rank, area), 1) % rank == iota((2 * rank, area), 0) % rank).astype(bf16)
    held = [jnp.concatenate(split_f32(jnp.where(kept, coef[p], 0.0)), axis=1) for p in range(2)]
    sums = [jnp.zeros((clusters, area), f32) for _ in range(2)]
    for i in range(blocks):
        sources = jnp.sum(jnp.where(iota(square, 1) == cluster_of, col_ref[i:i + 1, :], 0), axis=1, keepdims=True)
        source_rows = sources % groups * CHUNKS + sources // groups
        pick = (iota(square, 1) == source_rows).astype(bf16)
        real, imag = [
            jnp.dot(jnp.dot(pick, part, preferred_element_type=f32).astype(bf16), spread, preferred_element_type=f32)
            for part in held]
        low, high = ordered[0, i], ordered[1, i]
        sums[0] += low * real - high * imag
        sums[1] += high * real + low * imag
    gather = (iota((area, rank), 0) // rank == iota((area, rank), 1)).astype(bf16)
    middle = []
    for part in sums:
        hi, lo = split_f32(part)
        short = jnp.dot(hi, gather, preferred_element_type=f32) + jnp.dot(lo, gather, preferred_element_type=f32)
        middle.append(jnp.where(kept, short, 0.0))
    real, imag = middle
    wait_left()
    for g in range(groups):
        rows = slice(g * CHUNKS, (g + 1) * CHUNKS)
        mixed = jnp.concatenate([
            jnp.concatenate([real[rows], -imag[rows]], axis=1),
            jnp.concatenate([imag[rows], real[rows]], axis=1)], axis=0)
        masked = jnp.concatenate([jnp.where(chunk_row == c, mixed, 0.0) for c in range(CHUNKS)], axis=1)
        masked = jnp.concatenate(split_f32(masked), axis=0)
        for j in range(3):
            basis = jnp.concatenate([left_ref[c * groups + g, q, j] for c in range(CHUNKS) for q in range(2)], axis=0)
            out = jnp.dot(masked, basis, preferred_element_type=f32)
            out = out[:2 * CHUNKS] + out[2 * CHUNKS:]
            image_ref[j, :, g * LEAF:(g + 1) * LEAF] = out.astype(bf16)


def gather_phase(zs, ys, image_ref, out_ref, local_sem, meanwhile, finish, sems):
    zsend, zrecv, ysend, yrecv, csend, crecv = sems
    z, y, core = place(zs, ys)
    me = index_of(z, y, core, ys)
    mine = pltpu.make_async_copy(image_ref, out_ref.at[me], local_sem)
    mine.start()
    copies = []

    def send(block, j, source, target, send_sem, recv_sem):
        copy = pltpu.make_async_remote_copy(
            src_ref=source.at[j], dst_ref=out_ref.at[block, j], send_sem=send_sem, recv_sem=recv_sem,
            device_id={"freq": target}, device_id_type=MESH)
        copy.start()
        copies.append(copy)

    other = index_of(z, y, 1 - core, ys)
    far = sorted(range(1, zs), key=lambda s: -min(s, zs - s))
    near = far[::-1]

    def pass_y(block, j, source, s):
        for step in range(1, ys):
            send(block, j, source, index_of(z, lax.rem(y + step, ys), core, ys),
                 ysend.at[step - 1, s, j], yrecv.at[step - 1, s, j])

    def arrived(block, j, recv_sem):
        pltpu.make_async_copy(out_ref.at[block, j], out_ref.at[block, j], recv_sem).wait()

    for j in range(3):
        for s in far:
            send(me, j, image_ref, index_of(lax.rem(z + s, zs), y, core, ys), zsend.at[s - 1, j], zrecv.at[s - 1, j])
        pass_y(me, j, image_ref, 0)
        send(me, j, image_ref, other, csend.at[0, 0, j], crecv.at[0, 0, j])
    meanwhile()

    def from_z(j):
        for s in near:
            block = index_of(lax.rem(z + zs - s, zs), y, core, ys)
            arrived(block, j, zrecv.at[s - 1, j])
            pass_y(block, j, out_ref.at[block], s)
            send(block, j, out_ref.at[block], other, csend.at[0, s, j], crecv.at[0, s, j])

    def from_y(j):
        for s in [0] + near:
            for step in range(1, ys):
                block = index_of(lax.rem(z + zs - s, zs), lax.rem(y + ys - step, ys), core, ys)
                arrived(block, j, yrecv.at[step - 1, s, j])
                send(block, j, out_ref.at[block], other, csend.at[step, s, j], crecv.at[step, s, j])

    def from_core(j):
        for s in [0] + near:
            for step in range(ys):
                block = index_of(lax.rem(z + zs - s, zs), lax.rem(y + ys - step, ys), 1 - core, ys)
                arrived(block, j, crecv.at[step, s, j])
        finish(j)

    from_z(0)
    from_z(1)
    from_y(0)
    from_z(2)
    from_y(1)
    mine.wait()
    from_core(0)
    from_y(2)
    from_core(1)
    from_core(2)
    for copy in copies:
        copy.wait_send()


def traction_kernel(zs, ys, *refs):
    ids_ref, rank_ref, col_ref, slip_hbm, right_hbm, coupling_hbm, left_hbm = refs[:7]
    traction_hbm, images, hi_ref, lo_ref = refs[7:11]
    slip, right, coupling, left, ordered, coef, image, fetch_sems, local_sem = refs[11:20]
    scatter_refs, scatter_sems, gather_sems = refs[20:27], refs[27:33], refs[33:]
    z, y, core = place(zs, ys)
    ready = greet(partners(z, y, core, zs, ys))
    for j in range(3):
        pltpu.make_async_copy(slip_hbm.at[j], slip.at[j], fetch_sems.at[j]).start()
    fetches = [
        pltpu.make_async_copy(source, target, fetch_sems.at[3 + at])
        for at, (source, target) in enumerate([(coupling_hbm, coupling), (right_hbm, right), (left_hbm, left)])]
    for fetch in fetches:
        fetch.start()

    def between():
        fetches[0].wait()
        reorder_coupling(coupling, ordered)

    spectrum = scatter_phase(zs, ys, ready, ids_ref[...], slip, fetch_sems, between, *scatter_refs, scatter_sems)
    fetches[1].wait()
    operator_phase(spectrum, right, ordered, left, fetches[2].wait, rank_ref[...], col_ref, image, coef)
    times = slip.shape[1]

    def meanwhile():
        hi_ref[...], lo_ref[...] = inverse_matrix(ids_ref[...], index_of(z, y, core, ys) * times, times)

    traction, width = slip, image.shape[2]
    stores = [pltpu.make_async_copy(traction.at[j], traction_hbm.at[j], fetch_sems.at[j]) for j in range(3)]

    def finish(j):
        x = images[:, j].reshape(-1, width)
        res = jnp.dot(hi_ref[...], x, preferred_element_type=jnp.float32)
        res += jnp.dot(lo_ref[...], x, preferred_element_type=jnp.float32)
        for c in range(CHUNKS):
            traction[j, :, c * width:(c + 1) * width] = res[c * times:(c + 1) * times]
        stores[j].start()

    gather_phase(zs, ys, image, images, local_sem, meanwhile, finish, gather_sems)
    for store in stores:
        store.wait()


def all_tractions(ids, ranks, cols, slip, right, coupling, left, zs, ys):
    times, n = slip.shape[1], zs * ys * 2
    clusters, rank, blocks = right.shape[0], right.shape[3], coupling.shape[1]
    block = (3, 2 * CHUNKS, slip.shape[2] // CHUNKS)
    f32, bf16 = jnp.float32, jnp.bfloat16
    high, many = max(ys - 1, 1), max(zs - 1, 1)
    middle = (high, zs) if ys > 1 else (1, 1)
    vmem, hbm = pl.BlockSpec(memory_space=pltpu.VMEM), pl.BlockSpec(memory_space=pl.ANY)
    matrix = pltpu.VMEM((CHUNKS * times, n * 2 * CHUNKS), bf16)
    dma = pltpu.SemaphoreType.DMA
    return pl.pallas_call(
        functools.partial(traction_kernel, zs, ys),
        out_shape=jax.ShapeDtypeStruct(slip.shape, f32),
        in_specs=[vmem, vmem, vmem, hbm, hbm, hbm, hbm],
        out_specs=hbm,
        scratch_shapes=[
            pltpu.VMEM((n,) + block, bf16),
            matrix,
            matrix,
            pltpu.VMEM(slip.shape, f32),
            pltpu.VMEM(right.shape, bf16),
            pltpu.VMEM(coupling.shape, bf16),
            pltpu.VMEM(left.shape, bf16),
            pltpu.VMEM((2, blocks, clusters, rank * rank), f32),
            pltpu.VMEM((2, clusters, rank), f32),
            pltpu.VMEM(block, bf16),
            dma((6,)),
            dma,
            pltpu.VMEM((zs * ys,) + block, f32),
            pltpu.VMEM((zs * ys,) + block, bf16),
            pltpu.VMEM((zs * ys,) + block, bf16),
            pltpu.VMEM(middle + block, bf16),
            pltpu.VMEM(middle + block, bf16),
            pltpu.VMEM((many,) + block, bf16),
            pltpu.VMEM((many,) + block, bf16),
            dma((zs,)), dma((zs,)), dma((high, zs)), dma((high, zs)), dma((many,)), dma((many,)),
            dma((many, 3)), dma((many, 3)), dma((high, zs, 3)), dma((high, zs, 3)), dma((ys, zs, 3)), dma((ys, zs, 3)),
        ],
        compiler_params=pltpu.CompilerParams(
            collective_id=0, has_side_effects=True, vmem_limit_bytes=60 * MIB),
        name="traction",
    )(ids, ranks, cols, slip, right, coupling, left)


def body(zs, ys, slip_history, frequency_ids, col_clusters, basis_ranks, left_basis, right_basis, coupling):
    ids = frequency_ids.reshape(1, -1)
    slip = jnp.transpose(slip_history, (1, 0, 2))
    right = jnp.transpose(right_basis[0], (0, 1, 3, 2, 4))
    left = jnp.transpose(left_basis[0], (0, 1, 3, 2, 4))
    traction = all_tractions(
        ids, basis_ranks, col_clusters.T, slip, right, coupling[0], left, zs, ys)
    return jnp.transpose(traction, (1, 0, 2))


def solution(mesh):
    ys = max(4 // mesh.shape["group"], 1)
    zs = mesh.shape["freq"] // (2 * ys)
    return jax.shard_map(
        functools.partial(body, zs, ys),
        mesh=mesh,
        in_specs=(
            P("freq", None, "group"),
            P(),
            P(),
            P("freq", "group"),
            P("freq", "group", None, None, None, None),
            P("freq", "group", None, None, None, None),
            P("freq", "group", None, None, None),
        ),
        out_specs=P("freq", None, "group"),
        check_vma=False,
    )
```

time: 57.3 us -> 49 us (0.86)
  Pallas kernels: 50.7 us -> 45 us
  local copies, waits for them, and re-layouts: 6.06 us -> 3.76 us
    pallas_call x4 -> x1, Pallas kernels: 50.7 us -> 45 us  [all_tractions(): pl.pallas_call(functools.partial(traction_kernel, zs, ys), out_shape=jax....]
    unnamed x16 -> x1, local copies, waits for them, and re-layouts: 6.06 us -> 3.76 us
where the time goes in v2:
time: 49 us; the launch traced here: 48.8 us
  Pallas kernels  45 us (92%)
  local copies, waits for them, and re-layouts  3.76 us (8%)
    pallas_call x1, Pallas kernels, all_tractions(): pl.pallas_call(functools.partial(traction_kernel, zs, ys), out_shape=jax....  45 us
    unnamed x1, local copies, waits for them, and re-layouts  3.76 us

profile of v2, /device:TPU:9, one launch (start us, length us, event | category | flops | bytes accessed | tf_op | source)
XLA Modules:
  0.0 48.8 jit_solution(4038264326454527983)
XLA Ops:
  0.0 45.0 %traction.1 = f32[3,32,8192]{2,1,0:T(8,128)} custom-call(s32[1,16]{1,0:T(1,128)} %bitcast.17, s32[1,64]{1,0:T(1,128)} %refs_1_.1, s32[8,64]{1,0:T(8,128)} %bitcast.16, f32[3,32,8192]{2,1,0:T(8,128)} %bitcast.12, bf16[64,2,3,32,128]{4,3,2,1,0:T(8,128)(2,1)} %bitcast.13, bf16[64,8,2,1024]{3,2,1,0:T(2,128)(2,1)} %bitcast.15, bf16[64,2,3,32,128]{4,3,2,1,0:T(8,128)(2,1)} %bitcast.14), custom_call_target="tpu_custom_call" | custom-call | tf_op jit(solution)/shard_map/traction/pallas_call | solution.py:359
  45.0 3.8 %copy.9 = f32[32,3,8192]{2,0,1:T(8,128)} copy(f32[32,3,8192]{2,0,1:T(8,128)} %bitcast.11) | data formatting | bytes 6291456

commit v3 on v2

--- a/solution.py
+++ b/solution.py
@@ -98,7 +98,9 @@
     order = [s % zs for s in order if s % zs] + [0]
     table_hi, table_lo = forward_matrix(ids, index_of(z, y, core, ys) * times, times)
     table = jnp.concatenate([table_hi, table_hi, table_lo], axis=1)
-    for j in range(3):
+    stage0, stage1, stage2 = {}, {}, {}
+
+    def transform(j):
         pltpu.make_async_copy(slip_ref.at[j], slip_ref.at[j], slip_sems.at[j]).wait()
         x = jnp.concatenate([slip_ref[j, :, c * width:(c + 1) * width] for c in range(CHUNKS)], axis=0)
         hi, lo = split_f32(x)
@@ -106,56 +108,72 @@
         res = jnp.dot(table, stack, preferred_element_type=jnp.float32)
         res = res.reshape(zs * ys, 2, 2 * CHUNKS, width)
         first, second = res[:, 0], res[:, 1]
-        own = jnp.where(core == 0, first, second)
-        other = jnp.where(core == 0, second, first)
-        acc[:, j] = own
-        send0[:, j] = other.astype(jnp.bfloat16)
-    ready()
-    stage0 = {}
-    for s in order:
-        at = lax.rem(z + s, zs)
-        rows = pl.ds(at * ys, ys)
-        stage0[s] = pltpu.make_async_remote_copy(
-            src_ref=send0.at[rows], dst_ref=recv0.at[rows], send_sem=ss0.at[s], recv_sem=rs0.at[s],
+        acc[:, j] = jnp.where(core == 0, first, second)
+        send0[:, j] = jnp.where(core == 0, second, first).astype(jnp.bfloat16)
+        if j == 0:
+            ready()
+        stage0[j] = pltpu.make_async_remote_copy(
+            src_ref=send0.at[:, j], dst_ref=recv0.at[:, j], send_sem=ss0.at[j], recv_sem=rs0.at[j],
             device_id={"freq": index_of(z, y, 1 - core, ys)}, device_id_type=MESH)
-        stage0[s].start()
-    stage1, stage2 = {}, {}
-    for s in order:
-        at = lax.rem(z + s, zs)
-        stage0[s].wait_recv()
+        stage0[j].start()
+
+    def to_y(j):
+        stage0[j].wait_recv()
         for step in range(1, ys):
             there = lax.rem(y + step, ys)
-            block = at * ys + there
-            send1[step - 1, at] = (acc[block] + recv0[block].astype(jnp.float32)).astype(jnp.bfloat16)
-            stage1[s, step] = pltpu.make_async_remote_copy(
-                src_ref=send1.at[step - 1, at], dst_ref=recv1.at[step - 1, at],
-                send_sem=ss1.at[step - 1, s], recv_sem=rs1.at[step - 1, s],
+            for at in range(zs):
+                block = at * ys + there
+                send1[step - 1, at, j] = (acc[block, j] + recv0[block, j].astype(jnp.float32)).astype(jnp.bfloat16)
+            stage1[step, j] = pltpu.make_async_remote_copy(
+                src_ref=send1.at[step - 1, :, j], dst_ref=recv1.at[step - 1, :, j],
+                send_sem=ss1.at[step - 1, j], recv_sem=rs1.at[step - 1, j],
                 device_id={"freq": index_of(z, there, core, ys)}, device_id_type=MESH)
-            stage1[s, step].start()
-    between()
-    for s in order:
-        at = lax.rem(z + s, zs)
-        block = at * ys + y
-        total = acc[block] + recv0[block].astype(jnp.float32)
+            stage1[step, j].start()
+
+    def to_z(j):
         for step in range(1, ys):
-            stage1[s, step].wait_recv()
-            total += recv1[step - 1, at].astype(jnp.float32)
-        if s:
-            send2[s - 1] = total.astype(jnp.bfloat16)
-            stage2[s] = pltpu.make_async_remote_copy(
-                src_ref=send2.at[s - 1], dst_ref=recv2.at[s - 1], send_sem=ss2.at[s - 1], recv_sem=rs2.at[s - 1],
-                device_id={"freq": index_of(at, y, core, ys)}, device_id_type=MESH)
-            stage2[s].start()
-    for s in order[:-1]:
-        stage2[s].wait_recv()
-        total += recv2[s - 1].astype(jnp.float32)
+            stage1[step, j].wait_recv()
+        for s in order:
+            at = lax.rem(z + s, zs)
+            block = at * ys + y
+            total = acc[block, j] + recv0[block, j].astype(jnp.float32)
+            for step in range(1, ys):
+                total += recv1[step - 1, at, j].astype(jnp.float32)
+            if s:
+                send2[s - 1, j] = total.astype(jnp.bfloat16)
+                stage2[s, j] = pltpu.make_async_remote_copy(
+                    src_ref=send2.at[s - 1, j], dst_ref=recv2.at[s - 1, j],
+                    send_sem=ss2.at[s - 1, j], recv_sem=rs2.at[s - 1, j],
+                    device_id={"freq": index_of(at, y, core, ys)}, device_id_type=MESH)
+                stage2[s, j].start()
+        return total
+
+    transform(0)
+    transform(1)
+    to_y(0)
+    transform(2)
+    to_y(1)
+    between(0, 1)
+    to_y(2)
+    between(1, 3)
+    totals = [to_z(0)]
+    between(3, 5)
+    totals.append(to_z(1))
+    between(5, 7)
+    totals.append(to_z(2))
+    between(7, 8)
+    for j in range(3):
+        for s in order[:-1]:
+            stage2[s, j].wait_recv()
+            totals[j] += recv2[s - 1, j].astype(jnp.float32)
+    total = jnp.stack(totals)
     for copies in (stage0, stage1, stage2):
         for copy in copies.values():
             copy.wait_send()
     return total
 
 
-def reorder_coupling(coupling_ref, ordered):
+def reorder_coupling(coupling_ref, ordered, begin, end):
     groups, blocks = coupling_ref.shape[0] // CHUNKS, coupling_ref.shape[1]
 
     def step(g, carry):
@@ -166,7 +184,7 @@
                 ordered[q, i, rows, :] = jnp.concatenate([part[q:q + 1] for part in found], axis=0)
         return carry
 
-    lax.fori_loop(0, groups, step, 0)
+    lax.fori_loop(begin, end, step, 0)
 
 
 def operator_phase(spectrum, right_ref, ordered, left_ref, wait_left, rank_row, col_ref, image_ref, coef):
@@ -318,9 +336,11 @@
     for fetch in fetches:
         fetch.start()
 
-    def between():
-        fetches[0].wait()
-        reorder_coupling(coupling, ordered)
+    def between(begin, end):
+        if begin == 0:
+            fetches[0].wait()
+        groups = coupling.shape[0] // CHUNKS
+        reorder_coupling(coupling, ordered, begin * groups // 8, end * groups // 8)
 
     spectrum = scatter_phase(zs, ys, ready, ids_ref[...], slip, fetch_sems, between, *scatter_refs, scatter_sems)
     fetches[1].wait()
@@ -381,7 +401,7 @@
             pltpu.VMEM(middle + block, bf16),
             pltpu.VMEM((many,) + block, bf16),
             pltpu.VMEM((many,) + block, bf16),
-            dma((zs,)), dma((zs,)), dma((high, zs)), dma((high, zs)), dma((many,)), dma((many,)),
+            dma((3,)), dma((3,)), dma((high, 3)), dma((high, 3)), dma((many, 3)), dma((many, 3)),
             dma((many, 3)), dma((many, 3)), dma((high, zs, 3)), dma((high, zs, 3)), dma((ys, zs, 3)), dma((ys, zs, 3)),
         ],
         compiler_params=pltpu.CompilerParams(

time: 49 us -> 49.9 us (1.018)
  Pallas kernels: 45 us -> 46 us
    pallas_call x1, Pallas kernels: 45 us -> 46 us  [all_tractions(): pl.pallas_call(functools.partial(traction_kernel, zs, ys), out_shape=jax....]
where the time goes in v3:
time: 49.9 us; the launch traced here: 49.7 us
  Pallas kernels  46 us (92%)
  local copies, waits for them, and re-layouts  3.76 us (8%)
    pallas_call x1, Pallas kernels, all_tractions(): pl.pallas_call(functools.partial(traction_kernel, zs, ys), out_shape=jax....  46 us
    unnamed x1, local copies, waits for them, and re-layouts  3.76 us

profile of v3, /device:TPU:9, one launch (start us, length us, event | category | flops | bytes accessed | tf_op | source)
XLA Modules:
  0.0 49.7 jit_solution(11773415659902022762)
XLA Ops:
  0.0 46.0 %traction.1 = f32[3,32,8192]{2,1,0:T(8,128)} custom-call(s32[1,16]{1,0:T(1,128)} %bitcast.17, s32[1,64]{1,0:T(1,128)} %refs_1_.1, s32[8,64]{1,0:T(8,128)} %bitcast.16, f32[3,32,8192]{2,1,0:T(8,128)} %bitcast.12, bf16[64,2,3,32,128]{4,3,2,1,0:T(8,128)(2,1)} %bitcast.13, bf16[64,8,2,1024]{3,2,1,0:T(2,128)(2,1)} %bitcast.15, bf16[64,2,3,32,128]{4,3,2,1,0:T(8,128)(2,1)} %bitcast.14), custom_call_target="tpu_custom_call" | custom-call | tf_op jit(solution)/shard_map/traction/pallas_call | solution.py:379
  46.0 3.8 %copy.9 = f32[32,3,8192]{2,0,1:T(8,128)} copy(f32[32,3,8192]{2,0,1:T(8,128)} %bitcast.11) | data formatting | bytes 6291456

commit v4 on v2

--- a/solution.py
+++ b/solution.py
@@ -132,8 +132,8 @@
                 send_sem=ss1.at[step - 1, s], recv_sem=rs1.at[step - 1, s],
                 device_id={"freq": index_of(z, there, core, ys)}, device_id_type=MESH)
             stage1[s, step].start()
-    between()
-    for s in order:
+    for position, s in enumerate(order):
+        between(8 * position // zs, 8 * (position + 1) // zs)
         at = lax.rem(z + s, zs)
         block = at * ys + y
         total = acc[block] + recv0[block].astype(jnp.float32)
@@ -155,7 +155,7 @@
     return total
 
 
-def reorder_coupling(coupling_ref, ordered):
+def reorder_coupling(coupling_ref, ordered, begin, end):
     groups, blocks = coupling_ref.shape[0] // CHUNKS, coupling_ref.shape[1]
 
     def step(g, carry):
@@ -166,7 +166,7 @@
                 ordered[q, i, rows, :] = jnp.concatenate([part[q:q + 1] for part in found], axis=0)
         return carry
 
-    lax.fori_loop(0, groups, step, 0)
+    lax.fori_loop(begin, end, step, 0)
 
 
 def operator_phase(spectrum, right_ref, ordered, left_ref, wait_left, rank_row, col_ref, image_ref, coef):
@@ -318,9 +318,11 @@
     for fetch in fetches:
         fetch.start()
 
-    def between():
-        fetches[0].wait()
-        reorder_coupling(coupling, ordered)
+    def between(begin, end):
+        if begin == 0 and end > 0:
+            fetches[0].wait()
+        groups = coupling.shape[0] // CHUNKS
+        reorder_coupling(coupling, ordered, begin * groups // 8, end * groups // 8)
 
     spectrum = scatter_phase(zs, ys, ready, ids_ref[...], slip, fetch_sems, between, *scatter_refs, scatter_sems)
     fetches[1].wait()

time: 49 us -> 49 us (level)
  no operation moved by 1% of the time
where the time goes in v4:
time: 49 us; the launch traced here: 48.8 us
  Pallas kernels  45 us (92%)
  local copies, waits for them, and re-layouts  3.76 us (8%)
    pallas_call x1, Pallas kernels, all_tractions(): pl.pallas_call(functools.partial(traction_kernel, zs, ys), out_shape=jax....  45 us
    unnamed x1, local copies, waits for them, and re-layouts  3.76 us

profile of v4, /device:TPU:9, one launch (start us, length us, event | category | flops | bytes accessed | tf_op | source)
XLA Modules:
  0.0 48.8 jit_solution(10041091967007258846)
XLA Ops:
  0.0 45.0 %traction.1 = f32[3,32,8192]{2,1,0:T(8,128)} custom-call(s32[1,16]{1,0:T(1,128)} %bitcast.17, s32[1,64]{1,0:T(1,128)} %refs_1_.1, s32[8,64]{1,0:T(8,128)} %bitcast.16, f32[3,32,8192]{2,1,0:T(8,128)} %bitcast.12, bf16[64,2,3,32,128]{4,3,2,1,0:T(8,128)(2,1)} %bitcast.13, bf16[64,8,2,1024]{3,2,1,0:T(2,128)(2,1)} %bitcast.15, bf16[64,2,3,32,128]{4,3,2,1,0:T(8,128)(2,1)} %bitcast.14), custom_call_target="tpu_custom_call" | custom-call | tf_op jit(solution)/shard_map/traction/pallas_call | solution.py:361
  45.0 3.8 %copy.9 = f32[32,3,8192]{2,0,1:T(8,128)} copy(f32[32,3,8192]{2,0,1:T(8,128)} %bitcast.11) | data formatting | bytes 6291456
